TPU v7x, 32 devices: a whole 2x2x4 slice. The times are simulated.
32 devices in a mesh: row: 4 (over y, x), col: 8 (over z, core).
Axes of the slice: x: 2, y: 2, z: 4, core: 2. Of those that a mesh axis runs over, the one named last changes fastest.
Arguments:
- galaxy: float32 [128, 256, 256], P('row', 'col'), may hold values from 0.03 to 32, as said below
- randoms: float32 [128, 256, 256], P('row', 'col'), may hold values from 0.5 to 4
- coverage: int32 [128, 256, 256], P('row', 'col'), may hold values from 0 to 1
- patch: int32 [128, 256, 256], P('row', 'col'), may hold values from 0 to 127
Outputs:
- contrast: float32 [128, 256, 256], P('row', 'col')
- patch_sums: float32 [4, 128], replicated
Inputs may be any that keep to these rules, and one draw needn't show every extreme that they name: `galaxy`: positive densities.
All inputs are finite; a program needn't handle non-finite values.
Results may differ from a plain program's by a relative error of at most 0.00016.
Values sent between devices are 32-bit elements; how exact they have to be, the bound alone decides.
A program may use at most 64 MiB of HBM per device.

v0:
```python
import functools

import jax
import jax.numpy as jnp
import ml_dtypes
import numpy as np
from jax import lax
from jax.experimental import pallas as pl
from jax.experimental.pallas import tpu as pltpu
from jax.sharding import PartitionSpec as P

RADIUS = 16
NPATCH = 128
LANES = 128
F32 = jnp.float32
BF16 = jnp.bfloat16
MESH = pl.DeviceIdType.MESH


def taps_np():
    offs = np.arange(-RADIUS, RADIUS + 1).astype(np.float32)
    sigma = RADIUS / 2.0
    vals = np.exp(-offs * offs / np.float32(2.0 * sigma * sigma)).astype(np.float32)
    return (vals / vals.sum(dtype=np.float32)).astype(np.float32)


def split_np(mat):
    high = mat.astype(ml_dtypes.bfloat16)
    low = (mat - high.astype(np.float32)).astype(ml_dtypes.bfloat16)
    return high, low


def band(outs, ins, shift):
    taps = taps_np()
    mat = np.zeros((outs, ins), np.float32)
    for o in range(outs):
        for j in range(-RADIUS, RADIUS + 1):
            i = o + j + shift
            if 0 <= i < ins:
                mat[o, i] = taps[j + RADIUS]
    return mat


def split(val):
    high = val.astype(BF16)
    low = (val - high.astype(F32)).astype(BF16)
    return high, low


def dot(a, b):
    return jnp.dot(a, b, preferred_element_type=F32)


def gather_sum(axis, size, buf, send, recv):
    me = lax.axis_index(axis)
    copies = []
    for k in range(1, size):
        copy = pltpu.make_async_remote_copy(
            src_ref=buf.at[me],
            dst_ref=buf.at[me],
            send_sem=send.at[k - 1],
            recv_sem=recv.at[k - 1],
            device_id={axis: lax.rem(me + k, size)},
            device_id_type=MESH,
        )
        copy.start()
        copies.append(copy)
    return copies


def add_up(copies, buf, size):
    for copy in copies:
        copy.wait()
    total = buf[0]
    for k in range(1, size):
        total = total + buf[k]
    return total


def kernel(
    rows, cols, scale,
    *refs,
):
    hbm, (contrast, sums), vmem = refs[:11], refs[11:13], refs[13:24]
    (
        xb, yb, acc, trow, tcol, srow, scol, rb, oh, rh, sin,
        sx, rx, sy, ry, srel, rrel, s1, r1, s2, r2, s3, r3, s4, r4,
    ) = refs[24:]
    gal, ran, cov, pat, thi, tlo, kxhi, kxlo, kyhi, kylo, rep = vmem
    X, Y, Z = gal.shape
    halves = Z // LANES
    W = RADIUS
    me_r = lax.axis_index("row")
    me_c = lax.axis_index("col")

    PX = 8
    slabs = X // PX
    def fetch(k, slab=None):
        at = slice(None) if slab is None else pl.ds(slab * PX, PX)
        return pltpu.make_async_copy(
            hbm[k].at[at], vmem[k].at[at], sin.at[k, 0 if slab is None else slab]
        )

    fetch(4).start()
    fetch(5).start()
    for i in range(slabs):
        fetch(0, i).start()
        fetch(1, i).start()
    for k in (6, 7, 2, 8, 9, 3, 10):
        fetch(k).start()

    barrier = pltpu.get_barrier_semaphore()
    for k in range(1, rows):
        pl.semaphore_signal(barrier, inc=1, device_id={"row": lax.rem(me_r + k, rows)}, device_id_type=MESH)
    for k in range(1, cols):
        pl.semaphore_signal(barrier, inc=1, device_id={"col": lax.rem(me_c + k, cols)}, device_id_type=MESH)
    fetch(4).wait()
    fetch(5).wait()

    relayed = rows == 4
    YP = Y // 2

    def xsrc(h, up, part):
        return xb.at[h, :, pl.ds(X if up else W, W), pl.ds(part * YP, YP)]

    def xdst(h, up, part):
        return xb.at[h, :, pl.ds(0 if up else X + W, W), pl.ds(part * YP, YP)]

    def xsend(src, dst, ssem, rsem, hop):
        return pltpu.make_async_remote_copy(
            src_ref=src, dst_ref=dst, send_sem=ssem, recv_sem=rsem,
            device_id={"row": lax.rem(me_r + (hop + rows), rows)}, device_id_type=MESH,
        )

    def xcopy(h, up, part):
        u = int(up)
        return xsend(xsrc(h, up, part), xdst(h, up, part), sx.at[h, u, part], rx.at[h, u, part], 1 if up else -1)

    def xfirst(h, up):
        return xsend(xsrc(h, up, 1), rb.at[h], sx.at[h, int(up), 1], rrel.at[h], 2 if up else -2)

    def xsecond(h, up):
        return xsend(rb.at[h], xdst(h, up, 1), srel.at[h], rx.at[h, int(up), 1], -1 if up else 1)

    def xeach(h, act):
        for part in (1, 0):
            for up in (False, True):
                has = me_r < rows - 1 if up else me_r > 0
                if relayed and part == 1:
                    turn = me_r == (1 if up else 2)

                    @pl.when(turn)
                    def _():
                        act(xfirst(h, up))

                    has = jnp.logical_and(has, jnp.logical_not(turn))

                @pl.when(has)
                def _():
                    act(xcopy(h, up, part))

    def relay(h, act):
        if relayed:
            for up in (False, True):
                @pl.when(me_r == (3 if up else 0))
                def _():
                    act(xsecond(h, up))

    def relay_on(h):
        if relayed:
            for up in (False, True):
                @pl.when(me_r == (3 if up else 0))
                def _():
                    xfirst(h, up).wait_recv()
                    xsecond(h, up).start()

    def xarrived(h, part):
        @pl.when(me_r > 0)
        def _():
            xcopy(h, True, part).wait_recv()

        @pl.when(me_r < rows - 1)
        def _():
            xcopy(h, False, part).wait_recv()

    def ycopy(h, up):
        own, far = ((Y, 0) if up else (W, Y + W))
        return pltpu.make_async_remote_copy(
            src_ref=yb.at[h, :, :, pl.ds(own, W)],
            dst_ref=yb.at[h, :, :, pl.ds(far, W)],
            send_sem=sy.at[h, int(up)],
            recv_sem=ry.at[h, int(up)],
            device_id={"col": lax.rem(me_c + (1 if up else cols - 1), cols)},
            device_id_type=MESH,
        )

    def xstart(h):
        xeach(h, lambda copy: copy.start())

    def xsent(h):
        xeach(h, lambda copy: copy.wait_send())

    for h in range(halves):
        lanes = pl.ds(h * LANES, LANES)

        def zstep(i, unused):
            for f, ref in enumerate((gal, ran)):
                high, low = split(ref[pl.ds(i * PX, PX)].reshape(PX * Y, Z))
                th = thi[:, lanes]
                val = dot(high, th) + dot(high, tlo[:, lanes]) + dot(low, th)
                xb[h, f, pl.ds(W + i * PX, PX)] = val.reshape(PX, Y, LANES)
            return unused

        for i in range(slabs):
            if h == 0:
                fetch(0, i).wait()
                fetch(1, i).wait()
            zstep(i, 0)
        if h == 0:
            pl.semaphore_wait(barrier, rows + cols - 2)
            xstart(h)

        @pl.when(me_r == 0)
        def _():
            xb[h, :, 0:W] = jnp.zeros((2, W, Y, LANES), F32)

        @pl.when(me_r == rows - 1)
        def _():
            xb[h, :, X + W:] = jnp.zeros((2, W, Y, LANES), F32)

        @pl.when(me_c == 0)
        def _():
            yb[h, :, :, 0:W] = jnp.zeros((2, X, W, LANES), F32)

        @pl.when(me_c == cols - 1)
        def _():
            yb[h, :, :, Y + W:] = jnp.zeros((2, X, W, LANES), F32)

    for k in (2, 3, 6, 7, 8, 9, 10):
        fetch(k).wait()

    def tstep(i, carry):
        m = cov[i].astype(F32)
        g = (m * gal[i]).reshape(Y // 8, 8, Z).sum(axis=0)
        r = (m * ran[i]).reshape(Y // 8, 8, Z).sum(axis=0)
        return carry[0] + g, carry[1] + r

    zero = jnp.zeros((8, Z), F32)
    tg, tr = lax.fori_loop(0, X, tstep, (zero, zero))
    for f, t in enumerate((tg, tr)):
        trow[me_r, f] = sum(t[:, k * LANES:(k + 1) * LANES] for k in range(Z // LANES))
    row_totals = gather_sum("row", rows, trow, s1, r1)

    acc[...] = jnp.zeros_like(acc)
    iota = lax.broadcasted_iota(jnp.int32, (8, 2 * LANES), 0)

    def pair(ref, h, i):
        lx, ys, lanes = i // (Y // 8), pl.ds(i % (Y // 8) * 8, 8), pl.ds(h * LANES, LANES)
        return jnp.concatenate([ref[2 * lx, ys, lanes], ref[2 * lx + 1, ys, lanes]], axis=1)

    def wide(v, s):
        return jnp.broadcast_to(v[s:s + 1], (8, 2 * LANES))

    def onehots(h):
        def step(i, unused):
            p = jnp.where(pair(cov, h, i) > 0, pair(pat, h, i), -1)
            phi, plo = p >> 4, p & 15
            for s in range(8):
                at = pl.ds(s * 2 * LANES, 2 * LANES)
                one = jnp.where(wide(phi, s) == iota, 1.0, 0.0)
                oh[h, i, :, at] = jnp.concatenate([one, one], axis=0).astype(BF16)
                lows = [jnp.where(wide(plo, s) == iota + k, 1.0, 0.0) for k in (0, 8)]
                rh[h, i, :, at] = jnp.concatenate(lows, axis=0).astype(BF16)
            return unused

        lax.fori_loop(0, X // 2 * (Y // 8), step, 0, unroll=2)

    def finish(h, alpha):
        lanes = pl.ds(h * LANES, LANES)

        def cstep(i, unused):
            x4 = pl.ds(i * 4, 4)
            both = jnp.concatenate(
                [yb[h, f, x4].reshape(4 * (Y + 2 * W), LANES) for f in range(2)], axis=1
            )
            high, low = split(both)
            kh = kyhi[...]
            val = dot(kh, high) + dot(kylo[...], high) + dot(kh, low)
            m = cov[x4, :, lanes].astype(F32).reshape(4 * Y, LANES)
            nbar = alpha * val[:, LANES:]
            weight = 1.0 / (1.0 + 2.0 * nbar)
            c = m * weight * (val[:, :LANES] / nbar - 1.0)
            contrast[x4, :, lanes] = c.reshape(4, Y, LANES)
            return unused

        lax.fori_loop(0, X // 4, cstep, 0, unroll=2)

        def pstep(i, unused):
            c = pair(contrast, h, i)
            terms = [oh[h, i]]
            power = c
            for q in range(3):
                high, low = split(power)
                high, low = high.astype(F32), low.astype(F32)
                terms.append(jnp.concatenate([
                    jnp.concatenate([wide(high, s), wide(low, s)], axis=0).astype(BF16)
                    for s in range(8)
                ], axis=1) * oh[h, i])
                power = power * c
            acc[...] += lax.dot_general(
                rh[h, i], jnp.concatenate(terms, axis=0), (((1,), (1,)), ((), ())),
                preferred_element_type=F32,
            )
            return unused

        lax.fori_loop(0, X // 2 * (Y // 8), pstep, 0, unroll=4)

    for h in range(halves):
        def xstep(t, unused):
            ys = pl.ds(t * 8, 8)
            both = jnp.concatenate(
                [xb[h, f, :, ys].reshape((X + 2 * W) * 8, LANES) for f in range(2)], axis=1
            )
            high, low = split(both)
            kh = kxhi[...]
            val = dot(kh, high) + dot(kxlo[...], high) + dot(kh, low)
            for f in range(2):
                yb[h, f, :, pl.ds(W + t * 8, 8)] = val[:, f * LANES:(f + 1) * LANES].reshape(X, 8, LANES)
            return unused

        if h == 0:
            relay_on(0)
            onehots(0)
        xarrived(h, 0)
        if h == 0:
            tcol[me_c] = add_up(row_totals, trow, rows)
            col_totals = gather_sum("col", cols, tcol, s2, r2)
        lax.fori_loop(0, W // 8, xstep, 0)

        @pl.when(me_c > 0)
        def _():
            ycopy(h, False).start()

        xarrived(h, 1)
        xsent(h)
        if h + 1 < halves:
            xstart(h + 1)
        lax.fori_loop(W // 8, Y // 8, xstep, 0)

        @pl.when(me_c < cols - 1)
        def _():
            ycopy(h, True).start()

        if h > 0:
            onehots(h)

        @pl.when(me_c > 0)
        def _():
            ycopy(h, True).wait_recv()

        @pl.when(me_c < cols - 1)
        def _():
            ycopy(h, False).wait_recv()

        if h + 1 < halves:
            relay_on(h + 1)
        if h == 0:
            tot = add_up(col_totals, tcol, cols)
            alpha = jnp.sum(tot[0], keepdims=True) / jnp.sum(tot[1], keepdims=True)
        finish(h, alpha)

    a = acc[...].T
    terms = [a[0:8]] + [a[16 * q:16 * q + 8] + a[16 * q + 8:16 * q + 16] for q in range(1, 4)]
    spread = jnp.dot(
        jnp.concatenate(terms, axis=0), rep[...],
        precision=lax.Precision.HIGHEST, preferred_element_type=F32,
    )
    patch_hi = lax.broadcasted_iota(jnp.int32, (8, NPATCH), 1) // 16
    own = patch_hi == lax.broadcasted_iota(jnp.int32, (8, NPATCH), 0)
    for q in range(4):
        part = jnp.where(own, spread[8 * q:8 * q + 8], 0.0)
        srow[me_r, q:q + 1] = jnp.sum(part, axis=0, keepdims=True)
    srow[me_r, 4:8] = jnp.zeros((4, NPATCH), F32)
    scol[me_c] = add_up(gather_sum("row", rows, srow, s3, r3), srow, rows)
    whole = add_up(gather_sum("col", cols, scol, s4, r4), scol, cols)
    sums[...] = whole[0:4] * scale

    for h in range(halves):
        relay(h, lambda copy: copy.wait_send())

        @pl.when(me_c > 0)
        def _():
            ycopy(h, False).wait_send()

        @pl.when(me_c < cols - 1)
        def _():
            ycopy(h, True).wait_send()


def local(galaxy, randoms, coverage, patch):
    rows, cols = lax.axis_size("row"), lax.axis_size("col")
    X, Y, Z = galaxy.shape
    halves = Z // LANES
    W = RADIUS
    scale = NPATCH / (X * rows * Y * cols * Z)
    tz = split_np(band(Z, Z, 0).T)
    kx = split_np(np.kron(band(X, X + 2 * W, W), np.eye(8, dtype=np.float32)))
    ky = split_np(np.kron(np.eye(4, dtype=np.float32), band(Y, Y + 2 * W, W)))
    rep = (np.arange(NPATCH)[None, :] % 16 == np.arange(16)[:, None]).astype(np.float32)
    consts = [jnp.asarray(v) for v in (*tz, *kx, *ky, rep)]
    args = (galaxy, randoms, coverage, patch, *consts)
    vmem = pl.BlockSpec(memory_space=pltpu.VMEM)
    dma = pltpu.SemaphoreType.DMA
    contrast, sums = pl.pallas_call(
        functools.partial(kernel, rows, cols, scale),
        out_shape=(
            jax.ShapeDtypeStruct((X, Y, Z), F32),
            jax.ShapeDtypeStruct((4, NPATCH), F32),
        ),
        in_specs=[pl.BlockSpec(memory_space=pl.ANY)] * 11,
        out_specs=(vmem, vmem),
        scratch_shapes=[pltpu.VMEM(v.shape, v.dtype) for v in args] + [
            pltpu.VMEM((halves, 2, X + 2 * W, Y, LANES), F32),
            pltpu.VMEM((halves, 2, X, Y + 2 * W, LANES), F32),
            pltpu.VMEM((16, 64), F32),
            pltpu.VMEM((rows, 2, 8, LANES), F32),
            pltpu.VMEM((cols, 2, 8, LANES), F32),
            pltpu.VMEM((rows, 8, NPATCH), F32),
            pltpu.VMEM((cols, 8, NPATCH), F32),
            pltpu.VMEM((halves, 2, W, Y // 2, LANES), F32),
            pltpu.VMEM((halves, X // 2 * (Y // 8), 16, 16 * LANES), BF16),
            pltpu.VMEM((halves, X // 2 * (Y // 8), 16, 16 * LANES), BF16),
            dma((11, X // 8)),
            dma((halves, 2, 2)), dma((halves, 2, 2)), dma((halves, 2)), dma((halves, 2)),
            dma((halves,)), dma((halves,)),
            dma((rows - 1,)), dma((rows - 1,)), dma((cols - 1,)), dma((cols - 1,)),
            dma((rows - 1,)), dma((rows - 1,)), dma((cols - 1,)), dma((cols - 1,)),
        ],
        compiler_params=pltpu.CompilerParams(
            collective_id=0, has_side_effects=True, vmem_limit_bytes=60 * 1024 * 1024
        ),
    )(*args)
    return contrast, sums


def solution(mesh):
    spec = P("row", "col", None)
    return jax.shard_map(
        local, mesh=mesh, in_specs=(spec,) * 4, out_specs=(spec, P()), check_vma=False
    )
```

profile of v0, /device:TPU:0, one launch (start us, length us, event | category | flops | bytes accessed | tf_op | source)
XLA Modules:
  0.0 71.8 jit_solution(10063357859331588299)
XLA Ops:
  0.6 68.3 %shard_map.122 = (f32[32,32,256]{2,1,0:T(8,128)}, f32[4,128]{1,0:T(4,128)}) custom-call(f32[32,32,256]{2,1,0:T(8,128)} %refs_0_.1, f32[32,32,256]{2,1,0:T(8,128)} %refs_1_.1, s32[32,32,256]{2,1,0:T(8,128)} %refs_2_.1, s32[32,32,256]{2,1,0:T(8,128)} %refs_3_.1, bf16[256,256]{1,0:T(8,128)(2,1)} %constant.14.clone.refs_4_, ...), custom_call_target="tpu_custom_call" | custom-call | tf_op jit(solution)/shard_map/pallas_call | solution.py:414
  68.9 0.0 copy-start
  68.9 2.3 %copy.15 = f32[32,32,256]{2,1,0:T(8,128)} copy(f32[32,32,256]{2,1,0:T(8,128)} %get-tuple-element.4) | data formatting | bytes 2097152
  71.2 0.0 copy-done
  71.2 0.6 copy.16
Async XLA Ops:
  68.9 2.3 %copy-start = (f32[4,128]{1,0:T(4,128)S(1)}, f32[4,128]{1,0:T(4,128)}, u32[]{:S(2)}) copy-start(f32[4,128]{1,0:T(4,128)} %get-tuple-element.5) | copy-start | bytes 6148
where the time goes:
time: 72 us; the launch traced here: 71.8 us
  Pallas kernels  68.3 us (95%)
  local copies, waits for them, and re-layouts  2.89 us (4%)
    pallas_call x1, Pallas kernels, local(): pl.pallas_call(functools.partial(kernel, rows, cols, scale), out_shape=(j...  68.3 us
    unnamed x4, local copies, waits for them, and re-layouts  2.89 us

commit v1 on v0

v1 whole, which is shorter than its diff:
```python
import functools

import jax
import jax.numpy as jnp
import ml_dtypes
import numpy as np
from jax import lax
from jax.experimental import pallas as pl
from jax.experimental.pallas import tpu as pltpu
from jax.sharding import PartitionSpec as P

RADIUS = 16
NPATCH = 128
LANES = 128
GROUP = 4
F32 = jnp.float32
BF16 = jnp.bfloat16
MESH = pl.DeviceIdType.MESH


def taps_np():
    offs = np.arange(-RADIUS, RADIUS + 1).astype(np.float32)
    sigma = RADIUS / 2.0
    vals = np.exp(-offs * offs / np.float32(2.0 * sigma * sigma)).astype(np.float32)
    return (vals / vals.sum(dtype=np.float32)).astype(np.float32)


def split_np(mat):
    high = mat.astype(ml_dtypes.bfloat16)
    low = (mat - high.astype(np.float32)).astype(ml_dtypes.bfloat16)
    return high, low


def band(outs, ins, shift):
    taps = taps_np()
    mat = np.zeros((outs, ins), np.float32)
    for o in range(outs):
        for j in range(-RADIUS, RADIUS + 1):
            i = o + j + shift
            if 0 <= i < ins:
                mat[o, i] = taps[j + RADIUS]
    return mat


def split(val):
    high = val.astype(BF16)
    low = (val - high.astype(F32)).astype(BF16)
    return high, low


def dot(a, b):
    return jnp.dot(a, b, preferred_element_type=F32)


def gather_sum(axis, size, buf, send, recv):
    me = lax.axis_index(axis)
    copies = []
    for k in range(1, size):
        copy = pltpu.make_async_remote_copy(
            src_ref=buf.at[me],
            dst_ref=buf.at[me],
            send_sem=send.at[k - 1],
            recv_sem=recv.at[k - 1],
            device_id={axis: lax.rem(me + k, size)},
            device_id_type=MESH,
        )
        copy.start()
        copies.append(copy)
    return copies


def add_up(copies, buf, size):
    for copy in copies:
        copy.wait()
    total = buf[0]
    for k in range(1, size):
        total = total + buf[k]
    return total


def kernel(
    rows, cols, scale,
    *refs,
):
    hbm, (contrast, sums), vmem = refs[:11], refs[11:13], refs[13:24]
    (
        xb, yb, acc, trow, tcol, srow, scol, rb, oh, rh, sin,
        sx, rx, sy, ry, srel, rrel, s1, r1, s2, r2, s3, r3, s4, r4,
    ) = refs[24:]
    gal, ran, cov, pat, thi, tlo, kxhi, kxlo, kyhi, kylo, rep = vmem
    X, Y, Z = gal.shape
    W = RADIUS
    tiles = Y // 8
    me_r = lax.axis_index("row")
    me_c = lax.axis_index("col")

    PX = 8
    slabs = X // PX
    def fetch(k, slab=None):
        at = slice(None) if slab is None else pl.ds(slab * PX, PX)
        return pltpu.make_async_copy(
            hbm[k].at[at], vmem[k].at[at], sin.at[k, 0 if slab is None else slab]
        )

    fetch(4).start()
    fetch(5).start()
    for i in range(slabs):
        fetch(0, i).start()
        fetch(1, i).start()
    for k in (2, 3, 8, 9, 6, 7, 10):
        fetch(k).start()

    barrier = pltpu.get_barrier_semaphore()
    for k in range(1, rows):
        pl.semaphore_signal(barrier, inc=1, device_id={"row": lax.rem(me_r + k, rows)}, device_id_type=MESH)
    for k in range(1, cols):
        pl.semaphore_signal(barrier, inc=1, device_id={"col": lax.rem(me_c + k, cols)}, device_id_type=MESH)
    fetch(4).wait()
    fetch(5).wait()

    relayed = rows == 4
    detour = tiles // 2 if relayed else 0

    def xsrc(h, up, t):
        return xb.at[h, :, pl.ds(X if up else W, W), pl.ds(t * 8, 8)]

    def xdst(h, up, t):
        return xb.at[h, :, pl.ds(0 if up else X + W, W), pl.ds(t * 8, 8)]

    def xsend(src, dst, ssem, rsem, hop):
        return pltpu.make_async_remote_copy(
            src_ref=src, dst_ref=dst, send_sem=ssem, recv_sem=rsem,
            device_id={"row": lax.rem(me_r + (hop + rows), rows)}, device_id_type=MESH,
        )

    def xcopy(h, up, t):
        u = int(up)
        return xsend(xsrc(h, up, t), xdst(h, up, t), sx.at[h, u, t], rx.at[h, u, t], 1 if up else -1)

    def xfirst(h, up, t):
        return xsend(xsrc(h, up, t), rb.at[h, t], sx.at[h, int(up), t], rrel.at[h, t], 2 if up else -2)

    def xsecond(h, up, t):
        return xsend(rb.at[h, t], xdst(h, up, t), srel.at[h, t], rx.at[h, int(up), t], -1 if up else 1)

    def xeach(h, t, act):
        for up in (False, True):
            has = me_r < rows - 1 if up else me_r > 0
            if t < detour:
                turn = me_r == (1 if up else 2)

                @pl.when(turn)
                def _():
                    act(xfirst(h, up, t))

                has = jnp.logical_and(has, jnp.logical_not(turn))

            @pl.when(has)
            def _():
                act(xcopy(h, up, t))

    def relay(h, t, act):
        if t < detour:
            for up in (False, True):
                @pl.when(me_r == (3 if up else 0))
                def _():
                    act(up)

    def relay_on(h, t):
        def go(up):
            xfirst(h, up, t).wait_recv()
            xsecond(h, up, t).start()

        relay(h, t, go)

    def xarrived(h, t):
        @pl.when(me_r > 0)
        def _():
            xcopy(h, True, t).wait_recv()

        @pl.when(me_r < rows - 1)
        def _():
            xcopy(h, False, t).wait_recv()

    def ycopy(h, up):
        own, far = ((Y, 0) if up else (W, Y + W))
        return pltpu.make_async_remote_copy(
            src_ref=yb.at[h, :, :, pl.ds(own, W)],
            dst_ref=yb.at[h, :, :, pl.ds(far, W)],
            send_sem=sy.at[h, int(up)],
            recv_sem=ry.at[h, int(up)],
            device_id={"col": lax.rem(me_c + (1 if up else cols - 1), cols)},
            device_id_type=MESH,
        )

    def yeach(h, up, act):
        @pl.when(me_c < cols - 1 if up else me_c > 0)
        def _():
            act(ycopy(h, up))

    def yarrived(h):
        @pl.when(me_c > 0)
        def _():
            ycopy(h, True).wait_recv()

        @pl.when(me_c < cols - 1)
        def _():
            ycopy(h, False).wait_recv()

    def xstart(h, t):
        xeach(h, t, lambda copy: copy.start())

    for h in range(2):
        @pl.when(me_r == 0)
        def _():
            xb[h, :, 0:W] = jnp.zeros((2, W, Y, LANES), F32)

        @pl.when(me_r == rows - 1)
        def _():
            xb[h, :, X + W:] = jnp.zeros((2, W, Y, LANES), F32)

        @pl.when(me_c == 0)
        def _():
            yb[h, :, :, 0:W] = jnp.zeros((2, X, W, LANES), F32)

        @pl.when(me_c == cols - 1)
        def _():
            yb[h, :, :, Y + W:] = jnp.zeros((2, X, W, LANES), F32)

    for i in range(slabs):
        fetch(0, i).wait()
        fetch(1, i).wait()
        for f, ref in enumerate((gal, ran)):
            high, low = split(ref[pl.ds(i * PX, PX)].reshape(PX * Y, Z))
            val = dot(high, thi[...]) + dot(high, tlo[...]) + dot(low, thi[...])
            xb[0, f, pl.ds(W + i * PX, PX)] = val[:, :LANES].reshape(PX, Y, LANES)
            yb[1, f, pl.ds(i * PX, PX), pl.ds(W, Y)] = val[:, LANES:].reshape(PX, Y, LANES)

    pl.semaphore_wait(barrier, rows + cols - 2)
    for t in range(tiles):
        xstart(0, t)
    for up in (False, True):
        yeach(1, up, lambda copy: copy.start())

    for k in (2, 3):
        fetch(k).wait()

    def tstep(i, carry):
        m = cov[i].astype(F32)
        g = (m * gal[i]).reshape(Y // 8, 8, Z).sum(axis=0)
        r = (m * ran[i]).reshape(Y // 8, 8, Z).sum(axis=0)
        return carry[0] + g, carry[1] + r

    zero = jnp.zeros((8, Z), F32)
    tg, tr = lax.fori_loop(0, X, tstep, (zero, zero))
    for f, t in enumerate((tg, tr)):
        trow[me_r, f] = sum(t[:, k * LANES:(k + 1) * LANES] for k in range(Z // LANES))
    row_totals = gather_sum("row", rows, trow, s1, r1)

    acc[...] = jnp.zeros_like(acc)
    groups = X // 2 * tiles // GROUP

    def members(h, n):
        for k in range(GROUP):
            i = n * GROUP + k
            yield (i // tiles, i % tiles) if h == 0 else (i % (X // 2), i // (X // 2))

    def cells(ref, h, n):
        parts = []
        for lx, t in members(h, n):
            at = pl.ds(pl.multiple_of(t * 8, 8), 8), pl.ds(h * LANES, LANES)
            parts += [ref[(2 * lx, *at)], ref[(2 * lx + 1, *at)]]
        return jnp.concatenate(parts, axis=1)

    def onehots(h, first, last):
        def step(n, unused):
            p = jnp.where(cells(cov, h, n) > 0, cells(pat, h, n), -1)
            phi, plo = p >> 5, p & 31

            def rows_of(a, b):
                return jnp.concatenate([a, b], axis=0).astype(BF16)

            def one(v, k):
                return jnp.where(v == k, 1.0, 0.0)

            for k in range(4):
                hit = one(phi, k)
                oh[h, n, pl.ds(16 * k, 16)] = rows_of(hit, hit)
            for k in range(16):
                rh[h, n, pl.ds(16 * k, 16)] = rows_of(one(plo, 2 * k), one(plo, 2 * k + 1))
            return unused

        lax.fori_loop(first, last, step, 0)

    def histogram(h, first, last):
        def step(n, unused):
            c = cells(contrast, h, n)
            hot = oh[h, n]
            terms = [hot]
            power = c
            for q in range(3):
                high, low = split(power)
                both = jnp.concatenate([high.astype(F32), low.astype(F32)], axis=0).astype(BF16)
                terms.append(jnp.concatenate([both] * 4, axis=0) * hot)
                power = power * c
            acc[...] += lax.dot_general(
                rh[h, n], jnp.concatenate(terms, axis=0), (((1,), (1,)), ((), ())),
                preferred_element_type=F32,
            )
            return unused

        lax.fori_loop(first, last, step, 0)

    def ypass(h, i):
        both = jnp.concatenate(
            [yb[h, f, pl.ds(i * 4, 4)].reshape(4 * (Y + 2 * W), LANES) for f in range(2)], axis=1
        )
        high, low = split(both)
        kh = kyhi[...]
        return dot(kh, high) + dot(kylo[...], high) + dot(kh, low)

    def xpass(h, t):
        ys = pl.ds(t * 8, 8)
        both = jnp.concatenate(
            [xb[h, f, :, ys].reshape((X + 2 * W) * 8, LANES) for f in range(2)], axis=1
        )
        high, low = split(both)
        kh = kxhi[...]
        return dot(kh, high) + dot(kxlo[...], high) + dot(kh, low)

    def contrast_of(val, m, alpha):
        nbar = alpha * val[:, LANES:]
        weight = 1.0 / (1.0 + 2.0 * nbar)
        return m * weight * (val[:, :LANES] / nbar - 1.0)

    half = groups // 2
    onehots(0, 0, half)
    for k in (8, 9):
        fetch(k).wait()
    yarrived(1)

    def yown(i, unused):
        val = ypass(1, i)
        for f in range(2):
            xb[1, f, pl.ds(W + i * 4, 4)] = val[:, f * LANES:(f + 1) * LANES].reshape(4, Y, LANES)
        return unused

    lax.fori_loop(0, X // 4, yown, 0, unroll=2)
    for t in range(detour):
        relay_on(0, t)
    tcol[me_c] = add_up(row_totals, trow, rows)
    col_totals = gather_sum("col", cols, tcol, s2, r2)
    for t in range(tiles):
        xstart(1, t)
    onehots(0, half, groups)
    onehots(1, 0, groups)
    for t in range(detour):
        relay_on(1, t)
    tot = add_up(col_totals, tcol, cols)
    alpha = jnp.sum(tot[0], keepdims=True) / jnp.sum(tot[1], keepdims=True)
    for k in (6, 7, 10):
        fetch(k).wait()

    for t in range(tiles):
        xarrived(0, t)
        val = xpass(0, t)
        for f in range(2):
            yb[0, f, :, pl.ds(W + t * 8, 8)] = val[:, f * LANES:(f + 1) * LANES].reshape(X, 8, LANES)
        if t == W // 8 - 1:
            yeach(0, False, lambda copy: copy.start())
    yeach(0, True, lambda copy: copy.start())

    def last_of(h, t):
        lanes = pl.ds(h * LANES, LANES)
        xarrived(h, t)
        val = xpass(h, t)
        m = cov[:, pl.ds(t * 8, 8), lanes].astype(F32).reshape(X * 8, LANES)
        contrast[:, pl.ds(t * 8, 8), lanes] = contrast_of(val, m, alpha).reshape(X, 8, LANES)
        histogram(h, groups * t // tiles, groups * (t + 1) // tiles)

    def cstep(i, unused):
        val = ypass(0, i)
        x4, lanes = pl.ds(i * 4, 4), pl.ds(0, LANES)
        m = cov[x4, :, lanes].astype(F32).reshape(4 * Y, LANES)
        contrast[x4, :, lanes] = contrast_of(val, m, alpha).reshape(4, Y, LANES)
        return unused

    for t in range(tiles):
        if t == tiles // 2:
            yarrived(0)
            lax.fori_loop(0, X // 4, cstep, 0, unroll=2)
            histogram(0, 0, groups)
        last_of(1, t)

    a = acc[...]
    same = lax.broadcasted_iota(jnp.int32, a.shape, 0) % 8 == lax.broadcasted_iota(jnp.int32, a.shape, 1) % 8
    a = jnp.where(same, a, 0.0).reshape(32, 8, 256).sum(axis=1).T
    terms = []
    for q in range(4):
        for k in range(4):
            at = q * 64 + k * 16
            term = a[at:at + 8] if q == 0 else a[at:at + 8] + a[at + 8:at + 16]
            terms.append(jnp.sum(term, axis=0, keepdims=True))
    spread = jnp.dot(
        jnp.concatenate(terms, axis=0), rep[...],
        precision=lax.Precision.HIGHEST, preferred_element_type=F32,
    )
    own = lax.broadcasted_iota(jnp.int32, spread.shape, 1) // 32 == lax.broadcasted_iota(jnp.int32, spread.shape, 0) % 4
    spread = jnp.where(own, spread, 0.0)
    for q in range(4):
        srow[me_r, q:q + 1] = jnp.sum(spread[4 * q:4 * q + 4], axis=0, keepdims=True)
    srow[me_r, 4:8] = jnp.zeros((4, NPATCH), F32)
    scol[me_c] = add_up(gather_sum("row", rows, srow, s3, r3), srow, rows)
    whole = add_up(gather_sum("col", cols, scol, s4, r4), scol, cols)
    sums[...] = whole[0:4] * scale

    for h in range(2):
        for t in range(tiles):
            xeach(h, t, lambda copy: copy.wait_send())
            relay(h, t, lambda up: xsecond(h, up, t).wait_send())
        for up in (False, True):
            yeach(h, up, lambda copy: copy.wait_send())


def local(galaxy, randoms, coverage, patch):
    rows, cols = lax.axis_size("row"), lax.axis_size("col")
    X, Y, Z = galaxy.shape
    W = RADIUS
    tiles = Y // 8
    groups = X // 2 * tiles // GROUP
    scale = NPATCH / (X * rows * Y * cols * Z)
    tz = split_np(band(Z, Z, 0).T)
    kx = split_np(np.kron(band(X, X + 2 * W, W), np.eye(8, dtype=np.float32)))
    ky = split_np(np.kron(np.eye(4, dtype=np.float32), band(Y, Y + 2 * W, W)))
    rep = (np.arange(NPATCH)[None, :] % 32 == np.arange(32)[:, None]).astype(np.float32)
    consts = [jnp.asarray(v) for v in (*tz, *kx, *ky, rep)]
    args = (galaxy, randoms, coverage, patch, *consts)
    vmem = pl.BlockSpec(memory_space=pltpu.VMEM)
    dma = pltpu.SemaphoreType.DMA
    contrast, sums = pl.pallas_call(
        functools.partial(kernel, rows, cols, scale),
        out_shape=(
            pltpu.VMEM((X, Y, Z), F32),
            pltpu.VMEM((4, NPATCH), F32),
        ),
        in_specs=[pl.BlockSpec(memory_space=pl.ANY)] * 11,
        out_specs=(vmem, vmem),
        scratch_shapes=[pltpu.VMEM(v.shape, v.dtype) for v in args] + [
            pltpu.VMEM((2, 2, X + 2 * W, Y, LANES), F32),
            pltpu.VMEM((2, 2, X, Y + 2 * W, LANES), F32),
            pltpu.VMEM((256, 256), F32),
            pltpu.VMEM((rows, 2, 8, LANES), F32),
            pltpu.VMEM((cols, 2, 8, LANES), F32),
            pltpu.VMEM((rows, 8, NPATCH), F32),
            pltpu.VMEM((cols, 8, NPATCH), F32),
            pltpu.VMEM((2, tiles // 2, 2, W, 8, LANES), F32),
            pltpu.VMEM((2, groups, 64, 2 * LANES * GROUP), BF16),
            pltpu.VMEM((2, groups, 256, 2 * LANES * GROUP), BF16),
            dma((11, X // 8)),
            dma((2, 2, tiles)), dma((2, 2, tiles)), dma((2, 2)), dma((2, 2)),
            dma((2, tiles // 2)), dma((2, tiles // 2)),
            dma((rows - 1,)), dma((rows - 1,)), dma((cols - 1,)), dma((cols - 1,)),
            dma((rows - 1,)), dma((rows - 1,)), dma((cols - 1,)), dma((cols - 1,)),
        ],
        compiler_params=pltpu.CompilerParams(
            collective_id=0, has_side_effects=True, vmem_limit_bytes=56 * 1024 * 1024
        ),
    )(*args)
    return contrast, sums


def solution(mesh):
    spec = P("row", "col", None)
    return jax.shard_map(
        local, mesh=mesh, in_specs=(spec,) * 4, out_specs=(spec, P()), check_vma=False
    )
```

time: 72 us -> 65.8 us (0.914)
  Pallas kernels: 68.3 us -> 63.5 us
  local copies, waits for them, and re-layouts: 2.89 us -> 1.55 us
    pallas_call x1, Pallas kernels: 68.3 us -> 63.5 us  [local(): pl.pallas_call(functools.partial(kernel, rows, cols, scale), out_shape=(p...]
    unnamed x4 -> x2, local copies, waits for them, and re-layouts: 2.89 us -> 1.55 us
where the time goes in v1:
time: 65.8 us; the launch traced here: 65.7 us
  Pallas kernels  63.5 us (97%)
  local copies, waits for them, and re-layouts  1.55 us (2%)
    pallas_call x1, Pallas kernels, local(): pl.pallas_call(functools.partial(kernel, rows, cols, scale), out_shape=(p...  63.5 us
    unnamed x2, local copies, waits for them, and re-layouts  1.55 us

profile of v1, /device:TPU:0, one launch (start us, length us, event | category | flops | bytes accessed | tf_op | source)
XLA Modules:
  0.0 65.7 jit_solution(11129546161522545686)
XLA Ops:
  0.6 63.5 %shard_map.122 = (f32[32,32,256]{2,1,0:T(8,128)S(1)}, f32[4,128]{1,0:T(4,128)S(1)}) custom-call(f32[32,32,256]{2,1,0:T(8,128)} %refs_0_.1, f32[32,32,256]{2,1,0:T(8,128)} %refs_1_.1, s32[32,32,256]{2,1,0:T(8,128)} %refs_2_.1, s32[32,32,256]{2,1,0:T(8,128)} %refs_3_.1, bf16[256,256]{1,0:T(8,128)(2,1)} %constant.14.clone.refs_4_, ...), custom_call_target="tpu_custom_call" | custom-call | tf_op jit(solution)/shard_map/pallas_call | solution.py:440
  64.1 1.0 %copy.15 = f32[32,32,256]{2,1,0:T(8,128)} copy(f32[32,32,256]{2,1,0:T(8,128)S(1)} %get-tuple-element.2) | data formatting | bytes 2097152
  65.1 0.6 copy.16

commit v2 on v1

--- a/solution.py
+++ b/solution.py
@@ -12,7 +12,7 @@
 RADIUS = 16
 NPATCH = 128
 LANES = 128
-GROUP = 4
+GROUP = 16
 F32 = jnp.float32
 BF16 = jnp.bfloat16
 MESH = pl.DeviceIdType.MESH
@@ -272,7 +272,7 @@
             parts += [ref[(2 * lx, *at)], ref[(2 * lx + 1, *at)]]
         return jnp.concatenate(parts, axis=1)
 
-    def onehots(h, first, last):
+    def onehots(h):
         def step(n, unused):
             p = jnp.where(cells(cov, h, n) > 0, cells(pat, h, n), -1)
             phi, plo = p >> 5, p & 31
@@ -290,7 +290,7 @@
                 rh[h, n, pl.ds(16 * k, 16)] = rows_of(one(plo, 2 * k), one(plo, 2 * k + 1))
             return unused
 
-        lax.fori_loop(first, last, step, 0)
+        lax.fori_loop(0, groups, step, 0)
 
     def histogram(h, first, last):
         def step(n, unused):
@@ -309,7 +309,7 @@
             )
             return unused
 
-        lax.fori_loop(first, last, step, 0)
+        lax.fori_loop(first, last, step, 0, unroll=min(2, last - first))
 
     def ypass(h, i):
         both = jnp.concatenate(
@@ -333,8 +333,8 @@
         weight = 1.0 / (1.0 + 2.0 * nbar)
         return m * weight * (val[:, :LANES] / nbar - 1.0)
 
-    half = groups // 2
-    onehots(0, 0, half)
+    onehots(0)
+    onehots(1)
     for k in (8, 9):
         fetch(k).wait()
     yarrived(1)
@@ -348,14 +348,12 @@
     lax.fori_loop(0, X // 4, yown, 0, unroll=2)
     for t in range(detour):
         relay_on(0, t)
+    xstart(1, 0)
     tcol[me_c] = add_up(row_totals, trow, rows)
     col_totals = gather_sum("col", cols, tcol, s2, r2)
-    for t in range(tiles):
+    for t in range(1, tiles):
+        relay_on(1, t - 1)
         xstart(1, t)
-    onehots(0, half, groups)
-    onehots(1, 0, groups)
-    for t in range(detour):
-        relay_on(1, t)
     tot = add_up(col_totals, tcol, cols)
     alpha = jnp.sum(tot[0], keepdims=True) / jnp.sum(tot[1], keepdims=True)
     for k in (6, 7, 10):

time: 65.8 us -> 56.4 us (0.86)
  Pallas kernels: 63.5 us -> 54.1 us
    pallas_call x1, Pallas kernels: 63.5 us -> 54.1 us  [local(): pl.pallas_call(functools.partial(kernel, rows, cols, scale), out_shape=(p...]
where the time goes in v2:
time: 56.4 us; the launch traced here: 56.3 us
  Pallas kernels  54.1 us (96%)
  local copies, waits for them, and re-layouts  1.55 us (3%)
  between operations  0.64 us (1%)
    pallas_call x1, Pallas kernels, local(): pl.pallas_call(functools.partial(kernel, rows, cols, scale), out_shape=(p...  54.1 us
    unnamed x2, local copies, waits for them, and re-layouts  1.55 us

profile of v2, /device:TPU:0, one launch (start us, length us, event | category | flops | bytes accessed | tf_op | source)
XLA Modules:
  0.0 56.3 jit_solution(2714497407952441952)
XLA Ops:
  0.6 54.1 %shard_map.122 = (f32[32,32,256]{2,1,0:T(8,128)S(1)}, f32[4,128]{1,0:T(4,128)S(1)}) custom-call(f32[32,32,256]{2,1,0:T(8,128)} %refs_0_.1, f32[32,32,256]{2,1,0:T(8,128)} %refs_1_.1, s32[32,32,256]{2,1,0:T(8,128)} %refs_2_.1, s32[32,32,256]{2,1,0:T(8,128)} %refs_3_.1, bf16[256,256]{1,0:T(8,128)(2,1)} %constant.14.clone.refs_4_, ...), custom_call_target="tpu_custom_call" | custom-call | tf_op jit(solution)/shard_map/pallas_call | solution.py:438
  54.7 1.0 %copy.15 = f32[32,32,256]{2,1,0:T(8,128)} copy(f32[32,32,256]{2,1,0:T(8,128)S(1)} %get-tuple-element.2) | data formatting | bytes 2097152
  55.7 0.6 %copy.16 = f32[4,128]{1,0:T(4,128)} copy(f32[4,128]{1,0:T(4,128)S(1)} %get-tuple-element.3) | data formatting | bytes 4096

commit v3 on v2

--- a/solution.py
+++ b/solution.py
@@ -13,6 +13,7 @@
 NPATCH = 128
 LANES = 128
 GROUP = 16
+DIRECT = 32
 F32 = jnp.float32
 BF16 = jnp.bfloat16
 MESH = pl.DeviceIdType.MESH
@@ -78,13 +79,18 @@
     return total
 
 
+def shifts(rows, cols):
+    pairs = [(r, c) for r in range(rows) for c in range(cols) if (r, c) != (0, 0)]
+    return sorted(pairs, key=lambda rc: -(min(rc[0], 1) + min(rc[1], cols - rc[1])))
+
+
 def kernel(
     rows, cols, scale,
     *refs,
 ):
     hbm, (contrast, sums), vmem = refs[:11], refs[11:13], refs[13:24]
     (
-        xb, yb, acc, trow, tcol, srow, scol, rb, oh, rh, sin,
+        xb, yb, acc, trow, tcol, sall, scol, rb, oh, rh, sin,
         sx, rx, sy, ry, srel, rrel, s1, r1, s2, r2, s3, r3, s4, r4,
     ) = refs[24:]
     gal, ran, cov, pat, thi, tlo, kxhi, kxlo, kyhi, kylo, rep = vmem
@@ -182,30 +188,37 @@
         def _():
             xcopy(h, False, t).wait_recv()
 
-    def ycopy(h, up):
+    def ycopy(h, up, part):
         own, far = ((Y, 0) if up else (W, Y + W))
         return pltpu.make_async_remote_copy(
-            src_ref=yb.at[h, :, :, pl.ds(own, W)],
-            dst_ref=yb.at[h, :, :, pl.ds(far, W)],
-            send_sem=sy.at[h, int(up)],
-            recv_sem=ry.at[h, int(up)],
+            src_ref=yb.at[h, :, :, pl.ds(own + 8 * part, 8)],
+            dst_ref=yb.at[h, :, :, pl.ds(far + 8 * part, 8)],
+            send_sem=sy.at[h, int(up), part],
+            recv_sem=ry.at[h, int(up), part],
             device_id={"col": lax.rem(me_c + (1 if up else cols - 1), cols)},
             device_id_type=MESH,
         )
 
-    def yeach(h, up, act):
+    def yeach(h, up, part, act):
         @pl.when(me_c < cols - 1 if up else me_c > 0)
         def _():
-            act(ycopy(h, up))
+            act(ycopy(h, up, part))
+
+    def ystart(h, t):
+        for up in (False, True):
+            part = t - (tiles - W // 8 if up else 0)
+            if 0 <= part < W // 8:
+                yeach(h, up, part, lambda copy: copy.start())
 
     def yarrived(h):
-        @pl.when(me_c > 0)
-        def _():
-            ycopy(h, True).wait_recv()
-
-        @pl.when(me_c < cols - 1)
-        def _():
-            ycopy(h, False).wait_recv()
+        for part in range(W // 8):
+            @pl.when(me_c > 0)
+            def _():
+                ycopy(h, True, part).wait_recv()
+
+            @pl.when(me_c < cols - 1)
+            def _():
+                ycopy(h, False, part).wait_recv()
 
     def xstart(h, t):
         xeach(h, t, lambda copy: copy.start())
@@ -237,10 +250,10 @@
             yb[1, f, pl.ds(i * PX, PX), pl.ds(W, Y)] = val[:, LANES:].reshape(PX, Y, LANES)
 
     pl.semaphore_wait(barrier, rows + cols - 2)
+    xstart(0, 0)
+    xstart(0, 1)
     for t in range(tiles):
-        xstart(0, t)
-    for up in (False, True):
-        yeach(1, up, lambda copy: copy.start())
+        ystart(1, t)
 
     for k in (2, 3):
         fetch(k).wait()
@@ -333,40 +346,39 @@
         weight = 1.0 / (1.0 + 2.0 * nbar)
         return m * weight * (val[:, :LANES] / nbar - 1.0)
 
-    onehots(0)
-    onehots(1)
-    for k in (8, 9):
-        fetch(k).wait()
-    yarrived(1)
-
     def yown(i, unused):
         val = ypass(1, i)
         for f in range(2):
             xb[1, f, pl.ds(W + i * 4, 4)] = val[:, f * LANES:(f + 1) * LANES].reshape(4, Y, LANES)
         return unused
 
-    lax.fori_loop(0, X // 4, yown, 0, unroll=2)
-    for t in range(detour):
-        relay_on(0, t)
-    xstart(1, 0)
-    tcol[me_c] = add_up(row_totals, trow, rows)
-    col_totals = gather_sum("col", cols, tcol, s2, r2)
-    for t in range(1, tiles):
-        relay_on(1, t - 1)
-        xstart(1, t)
-    tot = add_up(col_totals, tcol, cols)
-    alpha = jnp.sum(tot[0], keepdims=True) / jnp.sum(tot[1], keepdims=True)
-    for k in (6, 7, 10):
-        fetch(k).wait()
-
-    for t in range(tiles):
+    def first_of(t):
         xarrived(0, t)
         val = xpass(0, t)
         for f in range(2):
             yb[0, f, :, pl.ds(W + t * 8, 8)] = val[:, f * LANES:(f + 1) * LANES].reshape(X, 8, LANES)
-        if t == W // 8 - 1:
-            yeach(0, False, lambda copy: copy.start())
-    yeach(0, True, lambda copy: copy.start())
+        ystart(0, t)
+
+    for t in range(2, tiles):
+        onehots(t - 2)
+        relay_on(0, t - 2)
+        xstart(0, t)
+    for k in (8, 9):
+        fetch(k).wait()
+    yarrived(1)
+    lax.fori_loop(0, X // 4, yown, 0, unroll=2)
+    xstart(1, 0)
+    tcol[me_c] = add_up(row_totals, trow, rows)
+    col_totals = gather_sum("col", cols, tcol, s2, r2)
+    for k in (6, 7, 10):
+        fetch(k).wait()
+    for t in range(tiles):
+        first_of(t)
+        relay_on(1, t)
+        if t + 1 < tiles:
+            xstart(1, t + 1)
+    tot = add_up(col_totals, tcol, cols)
+    alpha = jnp.sum(tot[0], keepdims=True) / jnp.sum(tot[1], keepdims=True)
 
     def last_of(h, t):
         lanes = pl.ds(h * LANES, LANES)
@@ -383,11 +395,10 @@
         contrast[x4, :, lanes] = contrast_of(val, m, alpha).reshape(4, Y, LANES)
         return unused
 
+    yarrived(0)
+    lax.fori_loop(0, X // 4, cstep, 0, unroll=2)
+    histogram(0, 0, groups)
     for t in range(tiles):
-        if t == tiles // 2:
-            yarrived(0)
-            lax.fori_loop(0, X // 4, cstep, 0, unroll=2)
-            histogram(0, 0, groups)
         last_of(1, t)
 
     a = acc[...]
@@ -405,19 +416,43 @@
     )
     own = lax.broadcasted_iota(jnp.int32, spread.shape, 1) // 32 == lax.broadcasted_iota(jnp.int32, spread.shape, 0) % 4
     spread = jnp.where(own, spread, 0.0)
-    for q in range(4):
-        srow[me_r, q:q + 1] = jnp.sum(spread[4 * q:4 * q + 4], axis=0, keepdims=True)
-    srow[me_r, 4:8] = jnp.zeros((4, NPATCH), F32)
-    scol[me_c] = add_up(gather_sum("row", rows, srow, s3, r3), srow, rows)
-    whole = add_up(gather_sum("col", cols, scol, s4, r4), scol, cols)
-    sums[...] = whole[0:4] * scale
+    mine = jnp.concatenate(
+        [jnp.sum(spread[4 * q:4 * q + 4], axis=0, keepdims=True) for q in range(4)]
+        + [jnp.zeros((4, NPATCH), F32)], axis=0,
+    )
+    if rows * cols <= DIRECT:
+        me = me_r * cols + me_c
+        sall[me] = mine
+        copies = []
+        for k, (kr, kc) in enumerate(shifts(rows, cols)):
+            copy = pltpu.make_async_remote_copy(
+                src_ref=sall.at[me, pl.ds(0, 4)],
+                dst_ref=sall.at[me, pl.ds(0, 4)],
+                send_sem=s3.at[k],
+                recv_sem=r3.at[k],
+                device_id={"row": lax.rem(me_r + kr, rows), "col": lax.rem(me_c + kc, cols)},
+                device_id_type=MESH,
+            )
+            copy.start()
+            copies.append(copy)
+        for copy in copies:
+            copy.wait_recv()
+        sums[...] = jnp.sum(sall[:, 0:4], axis=0) * scale
+        for copy in copies:
+            copy.wait_send()
+    else:
+        sall[me_r] = mine
+        scol[me_c] = add_up(gather_sum("row", rows, sall, s3, r3), sall, rows)
+        whole = add_up(gather_sum("col", cols, scol, s4, r4), scol, cols)
+        sums[...] = whole[0:4] * scale
 
     for h in range(2):
         for t in range(tiles):
             xeach(h, t, lambda copy: copy.wait_send())
             relay(h, t, lambda up: xsecond(h, up, t).wait_send())
         for up in (False, True):
-            yeach(h, up, lambda copy: copy.wait_send())
+            for part in range(W // 8):
+                yeach(h, up, part, lambda copy: copy.wait_send())
 
 
 def local(galaxy, randoms, coverage, patch):
@@ -426,6 +461,7 @@
     W = RADIUS
     tiles = Y // 8
     groups = X // 2 * tiles // GROUP
+    direct = (rows * cols if rows * cols <= DIRECT else rows) - 1
     scale = NPATCH / (X * rows * Y * cols * Z)
     tz = split_np(band(Z, Z, 0).T)
     kx = split_np(np.kron(band(X, X + 2 * W, W), np.eye(8, dtype=np.float32)))
@@ -449,16 +485,16 @@
             pltpu.VMEM((256, 256), F32),
             pltpu.VMEM((rows, 2, 8, LANES), F32),
             pltpu.VMEM((cols, 2, 8, LANES), F32),
-            pltpu.VMEM((rows, 8, NPATCH), F32),
+            pltpu.VMEM((direct + 1, 8, NPATCH), F32),
             pltpu.VMEM((cols, 8, NPATCH), F32),
             pltpu.VMEM((2, tiles // 2, 2, W, 8, LANES), F32),
             pltpu.VMEM((2, groups, 64, 2 * LANES * GROUP), BF16),
             pltpu.VMEM((2, groups, 256, 2 * LANES * GROUP), BF16),
             dma((11, X // 8)),
-            dma((2, 2, tiles)), dma((2, 2, tiles)), dma((2, 2)), dma((2, 2)),
+            dma((2, 2, tiles)), dma((2, 2, tiles)), dma((2, 2, W // 8)), dma((2, 2, W // 8)),
             dma((2, tiles // 2)), dma((2, tiles // 2)),
             dma((rows - 1,)), dma((rows - 1,)), dma((cols - 1,)), dma((cols - 1,)),
-            dma((rows - 1,)), dma((rows - 1,)), dma((cols - 1,)), dma((cols - 1,)),
+            dma((direct,)), dma((direct,)), dma((cols - 1,)), dma((cols - 1,)),
         ],
         compiler_params=pltpu.CompilerParams(
             collective_id=0, has_side_effects=True, vmem_limit_bytes=56 * 1024 * 1024

time: 56.4 us -> 53.1 us (0.941)
  Pallas kernels: 54.1 us -> 50.7 us
    pallas_call x1, Pallas kernels: 54.1 us -> 50.7 us  [local(): pl.pallas_call(functools.partial(kernel, rows, cols, scale), out_shape=(p...]
where the time goes in v3:
time: 53.1 us; the launch traced here: 52.9 us
  Pallas kernels  50.7 us (95%)
  local copies, waits for them, and re-layouts  1.55 us (3%)
  between operations  0.64 us (1%)
    pallas_call x1, Pallas kernels, local(): pl.pallas_call(functools.partial(kernel, rows, cols, scale), out_shape=(p...  50.7 us
    unnamed x2, local copies, waits for them, and re-layouts  1.55 us

profile of v3, /device:TPU:0, one launch (start us, length us, event | category | flops | bytes accessed | tf_op | source)
XLA Modules:
  0.0 52.9 jit_solution(963310666735399574)
XLA Ops:
  0.6 50.7 %shard_map.122 = (f32[32,32,256]{2,1,0:T(8,128)S(1)}, f32[4,128]{1,0:T(4,128)S(1)}) custom-call(f32[32,32,256]{2,1,0:T(8,128)} %refs_0_.1, f32[32,32,256]{2,1,0:T(8,128)} %refs_1_.1, s32[32,32,256]{2,1,0:T(8,128)} %refs_2_.1, s32[32,32,256]{2,1,0:T(8,128)} %refs_3_.1, bf16[256,256]{1,0:T(8,128)(2,1)} %constant.14.clone.refs_4_, ...), custom_call_target="tpu_custom_call" | custom-call | tf_op jit(solution)/shard_map/pallas_call | solution.py:474
  51.4 1.0 %copy.15 = f32[32,32,256]{2,1,0:T(8,128)} copy(f32[32,32,256]{2,1,0:T(8,128)S(1)} %get-tuple-element.2) | data formatting | bytes 2097152
  52.3 0.6 %copy.16 = f32[4,128]{1,0:T(4,128)} copy(f32[4,128]{1,0:T(4,128)S(1)} %get-tuple-element.3) | data formatting | bytes 4096

commit v4 on v3

--- a/solution.py
+++ b/solution.py
@@ -100,19 +100,17 @@
     me_r = lax.axis_index("row")
     me_c = lax.axis_index("col")
 
-    PX = 8
-    slabs = X // PX
-    def fetch(k, slab=None):
-        at = slice(None) if slab is None else pl.ds(slab * PX, PX)
-        return pltpu.make_async_copy(
-            hbm[k].at[at], vmem[k].at[at], sin.at[k, 0 if slab is None else slab]
-        )
-
+    def fetch(k, t=None):
+        at = slice(None) if t is None else (slice(None), pl.ds(t * 8, 8))
+        return pltpu.make_async_copy(hbm[k].at[at], vmem[k].at[at], sin.at[k, t or 0])
+
+    fetch(0, 0).start()
+    fetch(1, 0).start()
     fetch(4).start()
     fetch(5).start()
-    for i in range(slabs):
-        fetch(0, i).start()
-        fetch(1, i).start()
+    for t in range(1, tiles):
+        fetch(0, t).start()
+        fetch(1, t).start()
     for k in (2, 3, 8, 9, 6, 7, 10):
         fetch(k).start()
 
@@ -223,6 +221,20 @@
     def xstart(h, t):
         xeach(h, t, lambda copy: copy.start())
 
+    for t in range(tiles):
+        fetch(0, t).wait()
+        fetch(1, t).wait()
+        for f, ref in enumerate((gal, ran)):
+            high, low = split(ref[:, pl.ds(t * 8, 8)].reshape(X * 8, Z))
+            val = dot(high, thi[...]) + dot(high, tlo[...]) + dot(low, thi[...])
+            xb[0, f, pl.ds(W, X), pl.ds(t * 8, 8)] = val[:, :LANES].reshape(X, 8, LANES)
+            yb[1, f, :, pl.ds(W + t * 8, 8)] = val[:, LANES:].reshape(X, 8, LANES)
+        if t == 0:
+            pl.semaphore_wait(barrier, rows + cols - 2)
+        if t < 2:
+            xstart(0, t)
+        ystart(1, t)
+
     for h in range(2):
         @pl.when(me_r == 0)
         def _():
@@ -239,21 +251,6 @@
         @pl.when(me_c == cols - 1)
         def _():
             yb[h, :, :, Y + W:] = jnp.zeros((2, X, W, LANES), F32)
-
-    for i in range(slabs):
-        fetch(0, i).wait()
-        fetch(1, i).wait()
-        for f, ref in enumerate((gal, ran)):
-            high, low = split(ref[pl.ds(i * PX, PX)].reshape(PX * Y, Z))
-            val = dot(high, thi[...]) + dot(high, tlo[...]) + dot(low, thi[...])
-            xb[0, f, pl.ds(W + i * PX, PX)] = val[:, :LANES].reshape(PX, Y, LANES)
-            yb[1, f, pl.ds(i * PX, PX), pl.ds(W, Y)] = val[:, LANES:].reshape(PX, Y, LANES)
-
-    pl.semaphore_wait(barrier, rows + cols - 2)
-    xstart(0, 0)
-    xstart(0, 1)
-    for t in range(tiles):
-        ystart(1, t)
 
     for k in (2, 3):
         fetch(k).wait()
@@ -455,6 +452,16 @@
                 yeach(h, up, part, lambda copy: copy.wait_send())
 
 
+def store(contrast, sums, contrast_out, sums_out, sem):
+    step = contrast.shape[0] // 1
+    copies = [pltpu.make_async_copy(contrast.at[pl.ds(k * step, step)], contrast_out.at[pl.ds(k * step, step)], sem.at[k]) for k in range(1)]
+    copies.append(pltpu.make_async_copy(sums, sums_out, sem.at[1]))
+    for copy in copies:
+        copy.start()
+    for copy in copies:
+        copy.wait()
+
+
 def local(galaxy, randoms, coverage, patch):
     rows, cols = lax.axis_size("row"), lax.axis_size("col")
     X, Y, Z = galaxy.shape
@@ -490,7 +497,7 @@
             pltpu.VMEM((2, tiles // 2, 2, W, 8, LANES), F32),
             pltpu.VMEM((2, groups, 64, 2 * LANES * GROUP), BF16),
             pltpu.VMEM((2, groups, 256, 2 * LANES * GROUP), BF16),
-            dma((11, X // 8)),
+            dma((11, tiles)),
             dma((2, 2, tiles)), dma((2, 2, tiles)), dma((2, 2, W // 8)), dma((2, 2, W // 8)),
             dma((2, tiles // 2)), dma((2, tiles // 2)),
             dma((rows - 1,)), dma((rows - 1,)), dma((cols - 1,)), dma((cols - 1,)),
@@ -500,7 +507,16 @@
             collective_id=0, has_side_effects=True, vmem_limit_bytes=56 * 1024 * 1024
         ),
     )(*args)
-    return contrast, sums
+    return pl.pallas_call(
+        store,
+        out_shape=(
+            jax.ShapeDtypeStruct((X, Y, Z), F32),
+            jax.ShapeDtypeStruct((4, NPATCH), F32),
+        ),
+        in_specs=[pl.BlockSpec(memory_space=pl.ANY)] * 2,
+        out_specs=(pl.BlockSpec(memory_space=pl.ANY),) * 2,
+        scratch_shapes=[dma((1 + 1,))],
+    )(*(pltpu.with_memory_space_constraint(v, pltpu.VMEM) for v in (contrast, sums)))
 
 
 def solution(mesh):

time: 53.1 us -> 51.3 us (0.966)
  local copies, waits for them, and re-layouts: 1.55 us -> 0 us
    unnamed x2 -> x0, local copies, waits for them, and re-layouts: 1.55 us -> none
    pallas_call x1, Pallas kernels: 50.7 us -> 49.5 us  [local(): pl.pallas_call(functools.partial(kernel, rows, cols, scale), out_shape=(p...]
    pallas_call x0 -> x1, Pallas kernels: none -> 0.99 us  [local(): pl.pallas_call(store, out_shape=(jax.ShapeDtypeStruct((X, Y, Z), F32), ja...]
where the time goes in v4:
time: 51.3 us; the launch traced here: 51.2 us
  Pallas kernels  50.5 us (98%)
  between operations  0.64 us (1%)
    pallas_call x1, Pallas kernels, local(): pl.pallas_call(functools.partial(kernel, rows, cols, scale), out_shape=(p...  49.5 us

profile of v4, /device:TPU:0, one launch (start us, length us, event | category | flops | bytes accessed | tf_op | source)
XLA Modules:
  0.0 51.2 jit_solution(10624690285771065684)
XLA Ops:
  0.6 49.5 %shard_map.122 = (f32[32,32,256]{2,1,0:T(8,128)S(1)}, f32[4,128]{1,0:T(4,128)S(1)}) custom-call(f32[32,32,256]{2,1,0:T(8,128)} %refs_0_.1, f32[32,32,256]{2,1,0:T(8,128)} %refs_1_.1, s32[32,32,256]{2,1,0:T(8,128)} %refs_2_.1, s32[32,32,256]{2,1,0:T(8,128)} %refs_3_.1, bf16[256,256]{1,0:T(8,128)(2,1)} %constant.14.clone.refs_4_, ...), custom_call_target="tpu_custom_call" | custom-call | tf_op jit(solution)/shard_map/pallas_call | solution.py:481
  50.2 1.0 %shard_map.123 = (f32[32,32,256]{2,1,0:T(8,128)}, f32[4,128]{1,0:T(4,128)}) custom-call(f32[32,32,256]{2,1,0:T(8,128)S(1)} %get-tuple-element.4.contrast, f32[4,128]{1,0:T(4,128)S(1)} %get-tuple-element.5.sums), custom_call_target="tpu_custom_call" | custom-call | tf_op jit(solution)/shard_map/pallas_call | solution.py:510

commit v5 on v4

--- a/solution.py
+++ b/solution.py
@@ -147,17 +147,18 @@
     def xsecond(h, up, t):
         return xsend(rb.at[h, t], xdst(h, up, t), srel.at[h, t], rx.at[h, int(up), t], -1 if up else 1)
 
-    def xeach(h, t, act):
+    def xacross(h, t, act):
+        for up in (False, True):
+            if relayed:
+                @pl.when(me_r == (1 if up else 2))
+                def _():
+                    act((xfirst if t < detour else xcopy)(h, up, t))
+
+    def xalong(h, t, act):
         for up in (False, True):
             has = me_r < rows - 1 if up else me_r > 0
-            if t < detour:
-                turn = me_r == (1 if up else 2)
-
-                @pl.when(turn)
-                def _():
-                    act(xfirst(h, up, t))
-
-                has = jnp.logical_and(has, jnp.logical_not(turn))
+            if relayed:
+                has = jnp.logical_and(has, me_r != (1 if up else 2))
 
             @pl.when(has)
             def _():
@@ -218,8 +219,15 @@
             def _():
                 ycopy(h, False, part).wait_recv()
 
+    def xeach(h, t, act):
+        xacross(h, t, act)
+        xalong(h, t, act)
+
+    def begin(copy):
+        copy.start()
+
     def xstart(h, t):
-        xeach(h, t, lambda copy: copy.start())
+        xeach(h, t, begin)
 
     for t in range(tiles):
         fetch(0, t).wait()
@@ -270,21 +278,21 @@
     acc[...] = jnp.zeros_like(acc)
     groups = X // 2 * tiles // GROUP
 
-    def members(h, n):
-        for k in range(GROUP):
-            i = n * GROUP + k
+    def members(h, first, count):
+        for k in range(count):
+            i = first + k
             yield (i // tiles, i % tiles) if h == 0 else (i % (X // 2), i // (X // 2))
 
-    def cells(ref, h, n):
+    def cells(ref, h, first, count=GROUP):
         parts = []
-        for lx, t in members(h, n):
+        for lx, t in members(h, first, count):
             at = pl.ds(pl.multiple_of(t * 8, 8), 8), pl.ds(h * LANES, LANES)
             parts += [ref[(2 * lx, *at)], ref[(2 * lx + 1, *at)]]
         return jnp.concatenate(parts, axis=1)
 
     def onehots(h):
         def step(n, unused):
-            p = jnp.where(cells(cov, h, n) > 0, cells(pat, h, n), -1)
+            p = jnp.where(cells(cov, h, n * GROUP) > 0, cells(pat, h, n * GROUP), -1)
             phi, plo = p >> 5, p & 31
 
             def rows_of(a, b):
@@ -302,21 +310,29 @@
 
         lax.fori_loop(0, groups, step, 0)
 
+    def add_group(h, n, part=None):
+        if part is None:
+            at = slice(None)
+            c = cells(contrast, h, n * GROUP)
+        else:
+            at = pl.ds(pl.multiple_of(part * GROUP * LANES, GROUP * LANES), GROUP * LANES)
+            c = cells(contrast, h, n * GROUP + part * (GROUP // 2), GROUP // 2)
+        hot = oh[h, n, :, at]
+        terms = [hot]
+        power = c
+        for q in range(3):
+            high, low = split(power)
+            both = jnp.concatenate([high.astype(F32), low.astype(F32)], axis=0).astype(BF16)
+            terms.append(jnp.concatenate([both] * 4, axis=0) * hot)
+            power = power * c
+        acc[...] += lax.dot_general(
+            rh[h, n, :, at], jnp.concatenate(terms, axis=0), (((1,), (1,)), ((), ())),
+            preferred_element_type=F32,
+        )
+
     def histogram(h, first, last):
         def step(n, unused):
-            c = cells(contrast, h, n)
-            hot = oh[h, n]
-            terms = [hot]
-            power = c
-            for q in range(3):
-                high, low = split(power)
-                both = jnp.concatenate([high.astype(F32), low.astype(F32)], axis=0).astype(BF16)
-                terms.append(jnp.concatenate([both] * 4, axis=0) * hot)
-                power = power * c
-            acc[...] += lax.dot_general(
-                rh[h, n], jnp.concatenate(terms, axis=0), (((1,), (1,)), ((), ())),
-                preferred_element_type=F32,
-            )
+            add_group(h, n)
             return unused
 
         lax.fori_loop(first, last, step, 0, unroll=min(2, last - first))
@@ -373,9 +389,34 @@
         first_of(t)
         relay_on(1, t)
         if t + 1 < tiles:
-            xstart(1, t + 1)
+            if t == 0:
+                for k in range(1, tiles):
+                    xacross(1, k, begin)
+            xalong(1, t + 1, begin)
     tot = add_up(col_totals, tcol, cols)
     alpha = jnp.sum(tot[0], keepdims=True) / jnp.sum(tot[1], keepdims=True)
+
+    def half_of(t, upper):
+        ys, lanes = pl.ds(t * 8, 8), pl.ds(LANES, LANES)
+
+        @pl.when(jnp.logical_and(upper == 0, me_r > 0))
+        def _():
+            xcopy(1, True, t).wait_recv()
+
+        @pl.when(jnp.logical_and(upper == 1, me_r < rows - 1))
+        def _():
+            xcopy(1, False, t).wait_recv()
+
+        first = upper * W
+        both = jnp.concatenate(
+            [xb[1, f, pl.ds(first, 3 * W), ys].reshape(3 * W * 8, LANES) for f in range(2)], axis=1
+        )
+        high, low = split(both)
+        kh, kl = kxhi[0:W * 8, 0:3 * W * 8], kxlo[0:W * 8, 0:3 * W * 8]
+        val = dot(kh, high) + dot(kl, high) + dot(kh, low)
+        m = cov[pl.ds(first, W), ys, lanes].astype(F32).reshape(W * 8, LANES)
+        contrast[pl.ds(first, W), ys, lanes] = contrast_of(val, m, alpha).reshape(W, 8, LANES)
+        add_group(1, t, upper)
 
     def last_of(h, t):
         lanes = pl.ds(h * LANES, LANES)
@@ -395,8 +436,14 @@
     yarrived(0)
     lax.fori_loop(0, X // 4, cstep, 0, unroll=2)
     histogram(0, 0, groups)
-    for t in range(tiles):
-        last_of(1, t)
+    early = lax.rem(me_r, 2)
+    late = 1 - early
+    last_of(1, 0)
+    last_of(1, 1)
+    half_of(2, early)
+    half_of(3, early)
+    half_of(2, late)
+    half_of(3, late)
 
     a = acc[...]
     same = lax.broadcasted_iota(jnp.int32, a.shape, 0) % 8 == lax.broadcasted_iota(jnp.int32, a.shape, 1) % 8

time: 51.3 us -> 50.7 us (0.988)
  Pallas kernels: 50.5 us -> 49.9 us
    pallas_call x1, Pallas kernels: 49.5 us -> 48.9 us  [local(): pl.pallas_call(functools.partial(kernel, rows, cols, scale), out_shape=(p...]
where the time goes in v5:
time: 50.7 us; the launch traced here: 50.5 us
  Pallas kernels  49.9 us (98%)
  between operations  0.64 us (1%)
    pallas_call x1, Pallas kernels, local(): pl.pallas_call(functools.partial(kernel, rows, cols, scale), out_shape=(p...  48.9 us

profile of v5, /device:TPU:0, one launch (start us, length us, event | category | flops | bytes accessed | tf_op | source)
XLA Modules:
  0.0 50.5 jit_solution(614700465139013912)
XLA Ops:
  0.6 48.9 %shard_map.122 = (f32[32,32,256]{2,1,0:T(8,128)S(1)}, f32[4,128]{1,0:T(4,128)S(1)}) custom-call(f32[32,32,256]{2,1,0:T(8,128)} %refs_0_.1, f32[32,32,256]{2,1,0:T(8,128)} %refs_1_.1, s32[32,32,256]{2,1,0:T(8,128)} %refs_2_.1, s32[32,32,256]{2,1,0:T(8,128)} %refs_3_.1, bf16[256,256]{1,0:T(8,128)(2,1)} %constant.14.clone.refs_4_, ...), custom_call_target="tpu_custom_call" | custom-call | tf_op jit(solution)/shard_map/pallas_call | solution.py:528
  49.5 1.0 %shard_map.123 = (f32[32,32,256]{2,1,0:T(8,128)}, f32[4,128]{1,0:T(4,128)}) custom-call(f32[32,32,256]{2,1,0:T(8,128)S(1)} %get-tuple-element.4.contrast, f32[4,128]{1,0:T(4,128)S(1)} %get-tuple-element.5.sums), custom_call_target="tpu_custom_call" | custom-call | tf_op jit(solution)/shard_map/pallas_call | solution.py:557

commit v6 on v5

--- a/solution.py
+++ b/solution.py
@@ -104,6 +104,12 @@
         at = slice(None) if t is None else (slice(None), pl.ds(t * 8, 8))
         return pltpu.make_async_copy(hbm[k].at[at], vmem[k].at[at], sin.at[k, t or 0])
 
+    barrier = pltpu.get_barrier_semaphore()
+    for k in range(1, rows):
+        pl.semaphore_signal(barrier, inc=1, device_id={"row": lax.rem(me_r + k, rows)}, device_id_type=MESH)
+    for k in range(1, cols):
+        pl.semaphore_signal(barrier, inc=1, device_id={"col": lax.rem(me_c + k, cols)}, device_id_type=MESH)
+
     fetch(0, 0).start()
     fetch(1, 0).start()
     fetch(4).start()
@@ -113,12 +119,6 @@
         fetch(1, t).start()
     for k in (2, 3, 8, 9, 6, 7, 10):
         fetch(k).start()
-
-    barrier = pltpu.get_barrier_semaphore()
-    for k in range(1, rows):
-        pl.semaphore_signal(barrier, inc=1, device_id={"row": lax.rem(me_r + k, rows)}, device_id_type=MESH)
-    for k in range(1, cols):
-        pl.semaphore_signal(barrier, inc=1, device_id={"col": lax.rem(me_c + k, cols)}, device_id_type=MESH)
     fetch(4).wait()
     fetch(5).wait()
 
@@ -356,8 +356,7 @@
 
     def contrast_of(val, m, alpha):
         nbar = alpha * val[:, LANES:]
-        weight = 1.0 / (1.0 + 2.0 * nbar)
-        return m * weight * (val[:, :LANES] / nbar - 1.0)
+        return m * ((val[:, :LANES] - nbar) / (nbar * (1.0 + 2.0 * nbar)))
 
     def yown(i, unused):
         val = ypass(1, i)
@@ -433,12 +432,12 @@
         contrast[x4, :, lanes] = contrast_of(val, m, alpha).reshape(4, Y, LANES)
         return unused
 
+    early = lax.rem(me_r, 2)
+    late = 1 - early
+    last_of(1, 0)
     yarrived(0)
     lax.fori_loop(0, X // 4, cstep, 0, unroll=2)
     histogram(0, 0, groups)
-    early = lax.rem(me_r, 2)
-    late = 1 - early
-    last_of(1, 0)
     last_of(1, 1)
     half_of(2, early)
     half_of(3, early)
@@ -454,15 +453,9 @@
             at = q * 64 + k * 16
             term = a[at:at + 8] if q == 0 else a[at:at + 8] + a[at + 8:at + 16]
             terms.append(jnp.sum(term, axis=0, keepdims=True))
-    spread = jnp.dot(
-        jnp.concatenate(terms, axis=0), rep[...],
-        precision=lax.Precision.HIGHEST, preferred_element_type=F32,
-    )
-    own = lax.broadcasted_iota(jnp.int32, spread.shape, 1) // 32 == lax.broadcasted_iota(jnp.int32, spread.shape, 0) % 4
-    spread = jnp.where(own, spread, 0.0)
     mine = jnp.concatenate(
-        [jnp.sum(spread[4 * q:4 * q + 4], axis=0, keepdims=True) for q in range(4)]
-        + [jnp.zeros((4, NPATCH), F32)], axis=0,
+        [jnp.concatenate([terms[4 * q + k] for q in range(4)] + [jnp.zeros((4, 32), F32)], axis=0) for k in range(4)],
+        axis=1,
     )
     if rows * cols <= DIRECT:
         me = me_r * cols + me_c

time: 50.7 us -> 50.7 us (level)
  no operation moved by 1% of the time
where the time goes in v6:
time: 50.7 us; the launch traced here: 50.5 us
  Pallas kernels  49.9 us (98%)
  between operations  0.64 us (1%)
    pallas_call x1, Pallas kernels, local(): pl.pallas_call(functools.partial(kernel, rows, cols, scale), out_shape=(p...  48.9 us

profile of v6, /device:TPU:0, one launch (start us, length us, event | category | flops | bytes accessed | tf_op | source)
XLA Modules:
  0.0 50.5 jit_solution(14138442407919443274)
XLA Ops:
  0.6 48.9 %shard_map.122 = (f32[32,32,256]{2,1,0:T(8,128)S(1)}, f32[4,128]{1,0:T(4,128)S(1)}) custom-call(f32[32,32,256]{2,1,0:T(8,128)} %refs_0_.1, f32[32,32,256]{2,1,0:T(8,128)} %refs_1_.1, s32[32,32,256]{2,1,0:T(8,128)} %refs_2_.1, s32[32,32,256]{2,1,0:T(8,128)} %refs_3_.1, bf16[256,256]{1,0:T(8,128)(2,1)} %constant.14.clone.refs_4_, ...), custom_call_target="tpu_custom_call" | custom-call | tf_op jit(solution)/shard_map/pallas_call | solution.py:521
  49.5 1.0 %shard_map.123 = (f32[32,32,256]{2,1,0:T(8,128)}, f32[4,128]{1,0:T(4,128)}) custom-call(f32[32,32,256]{2,1,0:T(8,128)S(1)} %get-tuple-element.4.contrast, f32[4,128]{1,0:T(4,128)S(1)} %get-tuple-element.5.sums), custom_call_target="tpu_custom_call" | custom-call | tf_op jit(solution)/shard_map/pallas_call | solution.py:550

commit v7 on v6

--- a/solution.py
+++ b/solution.py
@@ -457,6 +457,15 @@
         [jnp.concatenate([terms[4 * q + k] for q in range(4)] + [jnp.zeros((4, 32), F32)], axis=0) for k in range(4)],
         axis=1,
     )
+    def drain():
+        for h in range(2):
+            for t in range(tiles):
+                xeach(h, t, lambda copy: copy.wait_send())
+                relay(h, t, lambda up: xsecond(h, up, t).wait_send())
+            for up in (False, True):
+                for part in range(W // 8):
+                    yeach(h, up, part, lambda copy: copy.wait_send())
+
     if rows * cols <= DIRECT:
         me = me_r * cols + me_c
         sall[me] = mine
@@ -472,24 +481,18 @@
             )
             copy.start()
             copies.append(copy)
+        drain()
+        for copy in copies:
+            copy.wait_send()
         for copy in copies:
             copy.wait_recv()
         sums[...] = jnp.sum(sall[:, 0:4], axis=0) * scale
-        for copy in copies:
-            copy.wait_send()
     else:
+        drain()
         sall[me_r] = mine
         scol[me_c] = add_up(gather_sum("row", rows, sall, s3, r3), sall, rows)
         whole = add_up(gather_sum("col", cols, scol, s4, r4), scol, cols)
         sums[...] = whole[0:4] * scale
-
-    for h in range(2):
-        for t in range(tiles):
-            xeach(h, t, lambda copy: copy.wait_send())
-            relay(h, t, lambda up: xsecond(h, up, t).wait_send())
-        for up in (False, True):
-            for part in range(W // 8):
-                yeach(h, up, part, lambda copy: copy.wait_send())
 
 
 def store(contrast, sums, contrast_out, sums_out, sem):

time: 50.7 us -> 50.6 us (level)
  no operation moved by 1% of the time
where the time goes in v7:
time: 50.6 us; the launch traced here: 50.4 us
  Pallas kernels  49.8 us (98%)
  between operations  0.64 us (1%)
    pallas_call x1, Pallas kernels, local(): pl.pallas_call(functools.partial(kernel, rows, cols, scale), out_shape=(p...  48.8 us

profile of v7, /device:TPU:0, one launch (start us, length us, event | category | flops | bytes accessed | tf_op | source)
XLA Modules:
  0.0 50.4 jit_solution(18287322512862849222)
XLA Ops:
  0.6 48.8 %shard_map.122 = (f32[32,32,256]{2,1,0:T(8,128)S(1)}, f32[4,128]{1,0:T(4,128)S(1)}) custom-call(f32[32,32,256]{2,1,0:T(8,128)} %refs_0_.1, f32[32,32,256]{2,1,0:T(8,128)} %refs_1_.1, s32[32,32,256]{2,1,0:T(8,128)} %refs_2_.1, s32[32,32,256]{2,1,0:T(8,128)} %refs_3_.1, bf16[256,256]{1,0:T(8,128)(2,1)} %constant.14.clone.refs_4_, ...), custom_call_target="tpu_custom_call" | custom-call | tf_op jit(solution)/shard_map/pallas_call | solution.py:524
  49.5 1.0 %shard_map.123 = (f32[32,32,256]{2,1,0:T(8,128)}, f32[4,128]{1,0:T(4,128)}) custom-call(f32[32,32,256]{2,1,0:T(8,128)S(1)} %get-tuple-element.4.contrast, f32[4,128]{1,0:T(4,128)S(1)} %get-tuple-element.5.sums), custom_call_target="tpu_custom_call" | custom-call | tf_op jit(solution)/shard_map/pallas_call | solution.py:553

commit v8 on v5

--- a/solution.py
+++ b/solution.py
@@ -260,6 +260,8 @@
         def _():
             yb[h, :, :, Y + W:] = jnp.zeros((2, X, W, LANES), F32)
 
+    for t in range(2, tiles):
+        xacross(0, t, begin)
     for k in (2, 3):
         fetch(k).wait()
 
@@ -375,7 +377,7 @@
     for t in range(2, tiles):
         onehots(t - 2)
         relay_on(0, t - 2)
-        xstart(0, t)
+        xalong(0, t, begin)
     for k in (8, 9):
         fetch(k).wait()
     yarrived(1)

time: 50.7 us -> 50.7 us (level)
  no operation moved by 1% of the time
where the time goes in v8:
time: 50.7 us; the launch traced here: 50.5 us
  Pallas kernels  49.9 us (98%)
  between operations  0.64 us (1%)
    pallas_call x1, Pallas kernels, local(): pl.pallas_call(functools.partial(kernel, rows, cols, scale), out_shape=(p...  48.9 us

profile of v8, /device:TPU:0, one launch (start us, length us, event | category | flops | bytes accessed | tf_op | source)
XLA Modules:
  0.0 50.5 jit_solution(10639189950112336452)
XLA Ops:
  0.6 48.9 %shard_map.122 = (f32[32,32,256]{2,1,0:T(8,128)S(1)}, f32[4,128]{1,0:T(4,128)S(1)}) custom-call(f32[32,32,256]{2,1,0:T(8,128)} %refs_0_.1, f32[32,32,256]{2,1,0:T(8,128)} %refs_1_.1, s32[32,32,256]{2,1,0:T(8,128)} %refs_2_.1, s32[32,32,256]{2,1,0:T(8,128)} %refs_3_.1, bf16[256,256]{1,0:T(8,128)(2,1)} %constant.14.clone.refs_4_, ...), custom_call_target="tpu_custom_call" | custom-call | tf_op jit(solution)/shard_map/pallas_call | solution.py:530
  49.5 1.0 %shard_map.123 = (f32[32,32,256]{2,1,0:T(8,128)}, f32[4,128]{1,0:T(4,128)}) custom-call(f32[32,32,256]{2,1,0:T(8,128)S(1)} %get-tuple-element.4.contrast, f32[4,128]{1,0:T(4,128)S(1)} %get-tuple-element.5.sums), custom_call_target="tpu_custom_call" | custom-call | tf_op jit(solution)/shard_map/pallas_call | solution.py:559

commit v9 on v7

--- a/solution.py
+++ b/solution.py
@@ -229,19 +229,32 @@
     def xstart(h, t):
         xeach(h, t, begin)
 
-    for t in range(tiles):
+    def zpass(t, h):
+        lanes = pl.ds(h * LANES, LANES)
+        for f, ref in enumerate((gal, ran)):
+            high, low = split(ref[:, pl.ds(t * 8, 8)].reshape(X * 8, Z))
+            th = thi[:, lanes]
+            val = (dot(high, th) + dot(high, tlo[:, lanes]) + dot(low, th)).reshape(X, 8, LANES)
+            if h == 0:
+                xb[0, f, pl.ds(W, X), pl.ds(t * 8, 8)] = val
+            else:
+                yb[1, f, :, pl.ds(W + t * 8, 8)] = val
+
+    for t in range(2):
         fetch(0, t).wait()
         fetch(1, t).wait()
-        for f, ref in enumerate((gal, ran)):
-            high, low = split(ref[:, pl.ds(t * 8, 8)].reshape(X * 8, Z))
-            val = dot(high, thi[...]) + dot(high, tlo[...]) + dot(low, thi[...])
-            xb[0, f, pl.ds(W, X), pl.ds(t * 8, 8)] = val[:, :LANES].reshape(X, 8, LANES)
-            yb[1, f, :, pl.ds(W + t * 8, 8)] = val[:, LANES:].reshape(X, 8, LANES)
+        zpass(t, 0)
         if t == 0:
             pl.semaphore_wait(barrier, rows + cols - 2)
-        if t < 2:
-            xstart(0, t)
+        xstart(0, t)
+    for t in range(tiles):
+        if t > 1:
+            fetch(0, t).wait()
+            fetch(1, t).wait()
+        zpass(t, 1)
         ystart(1, t)
+    for t in range(2, tiles):
+        zpass(t, 0)
 
     for h in range(2):
         @pl.when(me_r == 0)

time: 50.6 us -> 50.7 us (level)
  no operation moved by 1% of the time
where the time goes in v9:
time: 50.7 us; the launch traced here: 50.6 us
  Pallas kernels  49.8 us (98%)
  between operations  0.8 us (2%)
    pallas_call x1, Pallas kernels, local(): pl.pallas_call(functools.partial(kernel, rows, cols, scale), out_shape=(p...  48.8 us

profile of v9, /device:TPU:0, one launch (start us, length us, event | category | flops | bytes accessed | tf_op | source)
XLA Modules:
  0.0 50.6 jit_solution(320670444415019940)
XLA Ops:
  0.6 48.8 %shard_map.122 = (f32[32,32,256]{2,1,0:T(8,128)S(1)}, f32[4,128]{1,0:T(4,128)S(1)}) custom-call(f32[32,32,256]{2,1,0:T(8,128)} %refs_0_.1, f32[32,32,256]{2,1,0:T(8,128)} %refs_1_.1, s32[32,32,256]{2,1,0:T(8,128)} %refs_2_.1, s32[32,32,256]{2,1,0:T(8,128)} %refs_3_.1, bf16[256,256]{1,0:T(8,128)(2,1)} %constant.14.clone.refs_4_, ...), custom_call_target="tpu_custom_call" | custom-call | tf_op jit(solution)/shard_map/pallas_call | solution.py:537
  49.4 1.0 %shard_map.123 = (f32[32,32,256]{2,1,0:T(8,128)}, f32[4,128]{1,0:T(4,128)}) custom-call(f32[32,32,256]{2,1,0:T(8,128)S(1)} %get-tuple-element.4.contrast, f32[4,128]{1,0:T(4,128)S(1)} %get-tuple-element.5.sums), custom_call_target="tpu_custom_call" | custom-call | tf_op jit(solution)/shard_map/pallas_call | solution.py:566

commit v10 on v9

--- a/solution.py
+++ b/solution.py
@@ -273,6 +273,8 @@
         def _():
             yb[h, :, :, Y + W:] = jnp.zeros((2, X, W, LANES), F32)
 
+    for t in range(2, tiles):
+        xacross(0, t, begin)
     for k in (2, 3):
         fetch(k).wait()
 
@@ -387,7 +389,7 @@
     for t in range(2, tiles):
         onehots(t - 2)
         relay_on(0, t - 2)
-        xstart(0, t)
+        xalong(0, t, begin)
     for k in (8, 9):
         fetch(k).wait()
     yarrived(1)

time: 50.7 us -> 50.7 us (level)
  no operation moved by 1% of the time
where the time goes in v10:
time: 50.7 us; the launch traced here: 50.6 us
  Pallas kernels  49.8 us (98%)
  between operations  0.8 us (2%)
    pallas_call x1, Pallas kernels, local(): pl.pallas_call(functools.partial(kernel, rows, cols, scale), out_shape=(p...  48.8 us

profile of v10, /device:TPU:0, one launch (start us, length us, event | category | flops | bytes accessed | tf_op | source)
XLA Modules:
  0.0 50.6 jit_solution(1426707970606993449)
XLA Ops:
  0.6 48.8 %shard_map.122 = (f32[32,32,256]{2,1,0:T(8,128)S(1)}, f32[4,128]{1,0:T(4,128)S(1)}) custom-call(f32[32,32,256]{2,1,0:T(8,128)} %refs_0_.1, f32[32,32,256]{2,1,0:T(8,128)} %refs_1_.1, s32[32,32,256]{2,1,0:T(8,128)} %refs_2_.1, s32[32,32,256]{2,1,0:T(8,128)} %refs_3_.1, bf16[256,256]{1,0:T(8,128)(2,1)} %constant.14.clone.refs_4_, ...), custom_call_target="tpu_custom_call" | custom-call | tf_op jit(solution)/shard_map/pallas_call | solution.py:539
  49.4 1.0 %shard_map.123 = (f32[32,32,256]{2,1,0:T(8,128)}, f32[4,128]{1,0:T(4,128)}) custom-call(f32[32,32,256]{2,1,0:T(8,128)S(1)} %get-tuple-element.4.contrast, f32[4,128]{1,0:T(4,128)S(1)} %get-tuple-element.5.sums), custom_call_target="tpu_custom_call" | custom-call | tf_op jit(solution)/shard_map/pallas_call | solution.py:568
